TPU v7x, 32 devices: a whole 2x2x4 slice. The times are simulated.
32 devices in a mesh: tm: 16 (over z, x, core), space: 2 (over y).
Axes of the slice: x: 2, y: 2, z: 4, core: 2. Of those that a mesh axis runs over, the one named last changes fastest.
Arguments:
- forcing: float32 [64, 8, 128, 128], P('tm', 'space'), may hold values from -6 to 6
- conductivity: float32 [8, 128, 128], P('space'), may hold values from 0.5 to 2
- guess: float32 [16, 8, 128, 128], P('tm', 'space'), may hold values from -6 to 6
Outputs:
- solution: float32 [64, 8, 128, 128], P('tm', 'space')
All inputs are finite; a program needn't handle non-finite values.
Results may differ from a plain program's by a relative error of at most 0.00002.
Values sent between devices are 32-bit elements; how exact they have to be, the bound alone decides.
A program may use at most 64 MiB of HBM per device.

v0:
```python
import jax
import jax.numpy as jnp
from jax import lax
from jax.sharding import PartitionSpec as P

CF = 4


step_length = 0.1


def extended(block, sides, width):
    for axis, dim in sides:
        count = lax.axis_size(axis)
        forward = [(i, i + 1) for i in range(count - 1)]
        backward = [(target, source) for source, target in forward]
        low = lax.ppermute(
            lax.slice_in_dim(block, block.shape[dim] - width, None, axis=dim), axis, forward
        )
        high = lax.ppermute(lax.slice_in_dim(block, 0, width, axis=dim), axis, backward)
        block = jnp.concatenate([low, block, high], axis=dim)
    return block


def shifted(value, axis, steps):
    count = lax.axis_size(axis)
    pairs = [(source, (source + steps) % count) for source in range(count)]
    return lax.ppermute(value, axis, pairs)


def neighbours(field):
    middle = field[1:-1]
    total = field[:-2] + field[2:]
    total = total + jnp.roll(middle, 1, axis=1) + jnp.roll(middle, -1, axis=1)
    return total + jnp.roll(middle, 1, axis=2) + jnp.roll(middle, -1, axis=2)


def sweep_once(field, target, weight, scaled):
    return (target + weight * neighbours(field)) / scaled


def per_device(forcing, conductivity, guess):
    stacked = jnp.concatenate([conductivity[None], forcing], axis=0)
    widened = extended(stacked, (("space", 1),), 1)
    kappa_wide = widened[0]
    fine_weight = step_length * kappa_wide
    fine_scaled = 1.0 + 6.0 * fine_weight
    coarse_weight = CF * step_length * kappa_wide
    coarse_scaled = 1.0 + 6.0 * coarse_weight

    def advance(state, weight, scaled, source):
        padded = extended(state, (("space", 0),), 2)
        target = padded[1:-1]
        if source is not None:
            target = target + step_length * source
        first = sweep_once(padded, target, weight, scaled)
        return sweep_once(first, target[1:-1], weight[1:-1], scaled[1:-1])

    def fine_step(state, index):
        return advance(state, fine_weight, fine_scaled, widened[1 + index])

    def coarse_step(state):
        return advance(state, coarse_weight, coarse_scaled, None)

    def relax(anchor):
        states = [anchor]
        for index in range(1, CF):
            states.append(fine_step(states[-1], index))
        return states

    anchor = guess[0]
    states = relax(anchor)
    before = shifted(states[-1], "tm", 1)
    defect = fine_step(before, 0) - anchor
    count = lax.axis_size("tm")

    def relay(turn, carried):
        moved = shifted(carried, "tm", 1)
        return defect + coarse_step(moved)

    total = lax.fori_loop(0, count - 1, relay, defect)
    anchor = anchor + total
    return jnp.stack(relax(anchor), axis=0)


def solution(mesh):
    in_specs = (P("tm", "space", None, None), P("space", None, None), P("tm", "space", None, None))
    out_specs = P("tm", "space", None, None)
    return jax.shard_map(
        per_device, mesh=mesh, in_specs=in_specs, out_specs=out_specs, check_vma=False
    )
```

profile of v0, /device:TPU:0, one launch (start us, length us, event | category | flops | bytes accessed | tf_op | source)
XLA Modules:
  0.0 387.6 jit_solution(14018857676120985361)
XLA Ops:
  1.0 4.9 %collective-permute-start.3 = (f32[2,128,128]{2,1,0:T(8,128)S(1)}, f32[2,128,128]{2,1,0:T(8,128)S(1)}, u32[]{:S(2)}, u32[]{:S(2)}) collective-permute-start(f32[2,128,128]{2,1,0:T(8,128)S(1)} %get-tuple-element.193), channel_id=1, source_target_pairs={{0,1},{2,3},{4,5},{6,7},{8,9},{10,11},{12,13},{14,15},{16,17},{18,... | collective-permute-start | bytes 393224 | tf_op jit(solution)/shard_map/ppermute | solution.py:17
  8.3 4.6 %collective-permute-start.5 = (f32[5,1,128,128]{3,2,1,0:T(8,128)S(1)}, f32[5,1,128,128]{3,2,1,0:T(8,128)S(1)}, u32[]{:S(2)}, u32[]{:S(2)}) collective-permute-start(f32[5,1,128,128]{3,2,1,0:T(8,128)S(1)} %get-tuple-element.79), channel_id=1, source_target_pairs={{0,1},{2,3},{4,5},{6,7},{8,9},{10,11},{12,13},{14,15},{16,17},{18,... | collective-permute-start | bytes 983048 | tf_op jit(solution)/shard_map/ppermute | solution.py:17
  14.7 4.5 %collective-permute-done.5 = f32[5,1,128,128]{3,2,1,0:T(8,128)S(1)} collective-permute-done((f32[5,1,128,128]{3,2,1,0:T(8,128)S(1)}, f32[5,1,128,128]{3,2,1,0:T(8,128)S(1)}, u32[]{:S(2)}, u32[]{:S(2)}) %collective-permute-start.5) | collective-permute-done | bytes 327712 | tf_op jit(solution)/shard_map/ppermute | solution.py:17
  19.3 4.1 %collective-permute-done.6 = f32[5,1,128,128]{3,2,1,0:T(8,128)S(1)} collective-permute-done((f32[5,1,128,128]{3,2,1,0:T(8,128)S(1)}, f32[5,1,128,128]{3,2,1,0:T(8,128)S(1)}, u32[]{:S(2)}, u32[]{:S(2)}) %collective-permute-start.6) | collective-permute-done | bytes 327712 | tf_op jit(solution)/shard_map/ppermute | solution.py:20
  28.8 4.4 %collective-permute-done.8 = f32[2,128,128]{2,1,0:T(8,128)S(1)} collective-permute-done((f32[2,128,128]{2,1,0:T(8,128)S(1)}, f32[2,128,128]{2,1,0:T(8,128)S(1)}, u32[]{:S(2)}, u32[]{:S(2)}) %collective-permute-start.8) | collective-permute-done | bytes 131104 | tf_op jit(solution)/shard_map/ppermute | solution.py:20
  36.0 4.6 %collective-permute-start.9 = (f32[2,128,128]{2,1,0:T(8,128)S(1)}, f32[2,128,128]{2,1,0:T(8,128)S(1)}, u32[]{:S(2)}, u32[]{:S(2)}) collective-permute-start(f32[2,128,128]{2,1,0:T(8,128)S(1)} %get-tuple-element.189), channel_id=1, source_target_pairs={{0,1},{2,3},{4,5},{6,7},{8,9},{10,11},{12,13},{14,15},{16,17},{18,... | collective-permute-start | bytes 393224 | tf_op jit(solution)/shard_map/ppermute | solution.py:17
  41.5 1.5 collective-permute-done.9
  44.6 8.5 %collective-permute-done.11 = f32[4,128,128]{2,1,0:T(8,128)S(1)} collective-permute-done((f32[4,128,128]{2,1,0:T(8,128)S(1)}, f32[4,128,128]{2,1,0:T(8,128)S(1)}, u32[]{:S(2)}, u32[]{:S(2)}) %collective-permute-start.11) | collective-permute-done | bytes 262176 | tf_op jit(solution)/shard_map/ppermute | solution.py:28
  53.8 4.3 %collective-permute-start.12 = (f32[2,128,128]{2,1,0:T(8,128)}, f32[2,128,128]{2,1,0:T(8,128)S(1)}, u32[]{:S(2)}, u32[]{:S(2)}) collective-permute-start(f32[2,128,128]{2,1,0:T(8,128)} %get-tuple-element.188), channel_id=1, source_target_pairs={{0,1},{2,3},{4,5},{6,7},{8,9},{10,11},{12,13},{14,15},{16,17},{18,... | collective-permute-start | bytes 393224 | tf_op jit(solution)/shard_map/ppermute | solution.py:17
  59.5 1.5 collective-permute-done.12
  61.0 4.0 %collective-permute-done.13 = f32[2,128,128]{2,1,0:T(8,128)S(1)} collective-permute-done((f32[2,128,128]{2,1,0:T(8,128)S(1)}, f32[2,128,128]{2,1,0:T(8,128)S(1)}, u32[]{:S(2)}, u32[]{:S(2)}) %collective-permute-start.13) | collective-permute-done | bytes 131104 | tf_op jit(solution)/shard_map/ppermute | solution.py:20
  67.4 286.5 %while.10 = (s32[]{:T(128)}, f32[4,128,128]{2,1,0:T(8,128)S(1)}, f32[6,128,128]{2,1,0:T(8,128)S(1)}, f32[6,128,128]{2,1,0:T(8,128)S(1)}, f32[4,128,128]{2,1,0:T(8,128)S(1)}, /*index=5*/s32[]{:T(128)}) while((s32[]{:T(128)}, f32[4,128,128]{2,1,0:T(8,128)S(1)}, f32[6,128,128]{2,1,0:T(8,128)S(1)}, f32[6,128,128]{2,1,0:T(8,128)S(1)}, ...), condition=%wide.region_1.2_spmd, body=%wide.region_0.1_spmd.sunk | while | flops 2228226 | bytes 15466685 | solution.py:81
  67.5 8.5 %collective-permute-done = f32[4,128,128]{2,1,0:T(8,128)S(1)} collective-permute-done((f32[4,128,128]{2,1,0:T(8,128)S(1)}, f32[4,128,128]{2,1,0:T(8,128)S(1)}, u32[]{:S(2)}, u32[]{:S(2)}) %collective-permute-start) | collective-permute-done | bytes 262176 | tf_op jit(solution)/shard_map/while/body/eval_jaxpr/ppermute | solution.py:28
  79.4 1.5 collective-permute-done.1
  81.0 4.0 %collective-permute-done.2 = f32[2,128,128]{2,1,0:T(8,128)S(1)} collective-permute-done((f32[2,128,128]{2,1,0:T(8,128)S(1)}, f32[2,128,128]{2,1,0:T(8,128)S(1)}, u32[]{:S(2)}, u32[]{:S(2)}) %collective-permute-start.2) | collective-permute-done | bytes 131104 | tf_op jit(solution)/shard_map/while/body/eval_jaxpr/ppermute | solution.py:20
  86.6 8.5 %collective-permute-done = f32[4,128,128]{2,1,0:T(8,128)S(1)} collective-permute-done((f32[4,128,128]{2,1,0:T(8,128)S(1)}, f32[4,128,128]{2,1,0:T(8,128)S(1)}, u32[]{:S(2)}, u32[]{:S(2)}) %collective-permute-start) | collective-permute-done | bytes 262176 | tf_op jit(solution)/shard_map/while/body/eval_jaxpr/ppermute | solution.py:28
  98.5 1.5 collective-permute-done.1
  100.1 4.0 %collective-permute-done.2 = f32[2,128,128]{2,1,0:T(8,128)S(1)} collective-permute-done((f32[2,128,128]{2,1,0:T(8,128)S(1)}, f32[2,128,128]{2,1,0:T(8,128)S(1)}, u32[]{:S(2)}, u32[]{:S(2)}) %collective-permute-start.2) | collective-permute-done | bytes 131104 | tf_op jit(solution)/shard_map/while/body/eval_jaxpr/ppermute | solution.py:20
  105.7 8.5 %collective-permute-done = f32[4,128,128]{2,1,0:T(8,128)S(1)} collective-permute-done((f32[4,128,128]{2,1,0:T(8,128)S(1)}, f32[4,128,128]{2,1,0:T(8,128)S(1)}, u32[]{:S(2)}, u32[]{:S(2)}) %collective-permute-start) | collective-permute-done | bytes 262176 | tf_op jit(solution)/shard_map/while/body/eval_jaxpr/ppermute | solution.py:28
  117.6 1.5 collective-permute-done.1
  119.2 4.0 %collective-permute-done.2 = f32[2,128,128]{2,1,0:T(8,128)S(1)} collective-permute-done((f32[2,128,128]{2,1,0:T(8,128)S(1)}, f32[2,128,128]{2,1,0:T(8,128)S(1)}, u32[]{:S(2)}, u32[]{:S(2)}) %collective-permute-start.2) | collective-permute-done | bytes 131104 | tf_op jit(solution)/shard_map/while/body/eval_jaxpr/ppermute | solution.py:20
  124.8 8.5 %collective-permute-done = f32[4,128,128]{2,1,0:T(8,128)S(1)} collective-permute-done((f32[4,128,128]{2,1,0:T(8,128)S(1)}, f32[4,128,128]{2,1,0:T(8,128)S(1)}, u32[]{:S(2)}, u32[]{:S(2)}) %collective-permute-start) | collective-permute-done | bytes 262176 | tf_op jit(solution)/shard_map/while/body/eval_jaxpr/ppermute | solution.py:28
  136.7 1.5 collective-permute-done.1
  138.3 4.0 %collective-permute-done.2 = f32[2,128,128]{2,1,0:T(8,128)S(1)} collective-permute-done((f32[2,128,128]{2,1,0:T(8,128)S(1)}, f32[2,128,128]{2,1,0:T(8,128)S(1)}, u32[]{:S(2)}, u32[]{:S(2)}) %collective-permute-start.2) | collective-permute-done | bytes 131104 | tf_op jit(solution)/shard_map/while/body/eval_jaxpr/ppermute | solution.py:20
  143.9 8.5 %collective-permute-done = f32[4,128,128]{2,1,0:T(8,128)S(1)} collective-permute-done((f32[4,128,128]{2,1,0:T(8,128)S(1)}, f32[4,128,128]{2,1,0:T(8,128)S(1)}, u32[]{:S(2)}, u32[]{:S(2)}) %collective-permute-start) | collective-permute-done | bytes 262176 | tf_op jit(solution)/shard_map/while/body/eval_jaxpr/ppermute | solution.py:28
  155.8 1.5 collective-permute-done.1
  157.4 4.0 %collective-permute-done.2 = f32[2,128,128]{2,1,0:T(8,128)S(1)} collective-permute-done((f32[2,128,128]{2,1,0:T(8,128)S(1)}, f32[2,128,128]{2,1,0:T(8,128)S(1)}, u32[]{:S(2)}, u32[]{:S(2)}) %collective-permute-start.2) | collective-permute-done | bytes 131104 | tf_op jit(solution)/shard_map/while/body/eval_jaxpr/ppermute | solution.py:20
  163.0 8.5 %collective-permute-done = f32[4,128,128]{2,1,0:T(8,128)S(1)} collective-permute-done((f32[4,128,128]{2,1,0:T(8,128)S(1)}, f32[4,128,128]{2,1,0:T(8,128)S(1)}, u32[]{:S(2)}, u32[]{:S(2)}) %collective-permute-start) | collective-permute-done | bytes 262176 | tf_op jit(solution)/shard_map/while/body/eval_jaxpr/ppermute | solution.py:28
  174.9 1.5 collective-permute-done.1
  176.5 4.0 %collective-permute-done.2 = f32[2,128,128]{2,1,0:T(8,128)S(1)} collective-permute-done((f32[2,128,128]{2,1,0:T(8,128)S(1)}, f32[2,128,128]{2,1,0:T(8,128)S(1)}, u32[]{:S(2)}, u32[]{:S(2)}) %collective-permute-start.2) | collective-permute-done | bytes 131104 | tf_op jit(solution)/shard_map/while/body/eval_jaxpr/ppermute | solution.py:20
  182.1 8.5 %collective-permute-done = f32[4,128,128]{2,1,0:T(8,128)S(1)} collective-permute-done((f32[4,128,128]{2,1,0:T(8,128)S(1)}, f32[4,128,128]{2,1,0:T(8,128)S(1)}, u32[]{:S(2)}, u32[]{:S(2)}) %collective-permute-start) | collective-permute-done | bytes 262176 | tf_op jit(solution)/shard_map/while/body/eval_jaxpr/ppermute | solution.py:28
  194.0 1.5 collective-permute-done.1
  195.6 4.0 %collective-permute-done.2 = f32[2,128,128]{2,1,0:T(8,128)S(1)} collective-permute-done((f32[2,128,128]{2,1,0:T(8,128)S(1)}, f32[2,128,128]{2,1,0:T(8,128)S(1)}, u32[]{:S(2)}, u32[]{:S(2)}) %collective-permute-start.2) | collective-permute-done | bytes 131104 | tf_op jit(solution)/shard_map/while/body/eval_jaxpr/ppermute | solution.py:20
  201.2 8.5 %collective-permute-done = f32[4,128,128]{2,1,0:T(8,128)S(1)} collective-permute-done((f32[4,128,128]{2,1,0:T(8,128)S(1)}, f32[4,128,128]{2,1,0:T(8,128)S(1)}, u32[]{:S(2)}, u32[]{:S(2)}) %collective-permute-start) | collective-permute-done | bytes 262176 | tf_op jit(solution)/shard_map/while/body/eval_jaxpr/ppermute | solution.py:28
  213.1 1.5 collective-permute-done.1
  214.7 4.0 %collective-permute-done.2 = f32[2,128,128]{2,1,0:T(8,128)S(1)} collective-permute-done((f32[2,128,128]{2,1,0:T(8,128)S(1)}, f32[2,128,128]{2,1,0:T(8,128)S(1)}, u32[]{:S(2)}, u32[]{:S(2)}) %collective-permute-start.2) | collective-permute-done | bytes 131104 | tf_op jit(solution)/shard_map/while/body/eval_jaxpr/ppermute | solution.py:20
  220.3 8.5 %collective-permute-done = f32[4,128,128]{2,1,0:T(8,128)S(1)} collective-permute-done((f32[4,128,128]{2,1,0:T(8,128)S(1)}, f32[4,128,128]{2,1,0:T(8,128)S(1)}, u32[]{:S(2)}, u32[]{:S(2)}) %collective-permute-start) | collective-permute-done | bytes 262176 | tf_op jit(solution)/shard_map/while/body/eval_jaxpr/ppermute | solution.py:28
  232.2 1.5 collective-permute-done.1
  233.8 4.0 %collective-permute-done.2 = f32[2,128,128]{2,1,0:T(8,128)S(1)} collective-permute-done((f32[2,128,128]{2,1,0:T(8,128)S(1)}, f32[2,128,128]{2,1,0:T(8,128)S(1)}, u32[]{:S(2)}, u32[]{:S(2)}) %collective-permute-start.2) | collective-permute-done | bytes 131104 | tf_op jit(solution)/shard_map/while/body/eval_jaxpr/ppermute | solution.py:20
  239.4 8.5 %collective-permute-done = f32[4,128,128]{2,1,0:T(8,128)S(1)} collective-permute-done((f32[4,128,128]{2,1,0:T(8,128)S(1)}, f32[4,128,128]{2,1,0:T(8,128)S(1)}, u32[]{:S(2)}, u32[]{:S(2)}) %collective-permute-start) | collective-permute-done | bytes 262176 | tf_op jit(solution)/shard_map/while/body/eval_jaxpr/ppermute | solution.py:28
  251.3 1.5 collective-permute-done.1
  252.9 4.0 %collective-permute-done.2 = f32[2,128,128]{2,1,0:T(8,128)S(1)} collective-permute-done((f32[2,128,128]{2,1,0:T(8,128)S(1)}, f32[2,128,128]{2,1,0:T(8,128)S(1)}, u32[]{:S(2)}, u32[]{:S(2)}) %collective-permute-start.2) | collective-permute-done | bytes 131104 | tf_op jit(solution)/shard_map/while/body/eval_jaxpr/ppermute | solution.py:20
  258.5 8.5 %collective-permute-done = f32[4,128,128]{2,1,0:T(8,128)S(1)} collective-permute-done((f32[4,128,128]{2,1,0:T(8,128)S(1)}, f32[4,128,128]{2,1,0:T(8,128)S(1)}, u32[]{:S(2)}, u32[]{:S(2)}) %collective-permute-start) | collective-permute-done | bytes 262176 | tf_op jit(solution)/shard_map/while/body/eval_jaxpr/ppermute | solution.py:28
  270.4 1.5 collective-permute-done.1
  272.0 4.0 %collective-permute-done.2 = f32[2,128,128]{2,1,0:T(8,128)S(1)} collective-permute-done((f32[2,128,128]{2,1,0:T(8,128)S(1)}, f32[2,128,128]{2,1,0:T(8,128)S(1)}, u32[]{:S(2)}, u32[]{:S(2)}) %collective-permute-start.2) | collective-permute-done | bytes 131104 | tf_op jit(solution)/shard_map/while/body/eval_jaxpr/ppermute | solution.py:20
  277.6 8.5 %collective-permute-done = f32[4,128,128]{2,1,0:T(8,128)S(1)} collective-permute-done((f32[4,128,128]{2,1,0:T(8,128)S(1)}, f32[4,128,128]{2,1,0:T(8,128)S(1)}, u32[]{:S(2)}, u32[]{:S(2)}) %collective-permute-start) | collective-permute-done | bytes 262176 | tf_op jit(solution)/shard_map/while/body/eval_jaxpr/ppermute | solution.py:28
  289.5 1.5 collective-permute-done.1
  291.1 4.0 %collective-permute-done.2 = f32[2,128,128]{2,1,0:T(8,128)S(1)} collective-permute-done((f32[2,128,128]{2,1,0:T(8,128)S(1)}, f32[2,128,128]{2,1,0:T(8,128)S(1)}, u32[]{:S(2)}, u32[]{:S(2)}) %collective-permute-start.2) | collective-permute-done | bytes 131104 | tf_op jit(solution)/shard_map/while/body/eval_jaxpr/ppermute | solution.py:20
  296.7 8.5 %collective-permute-done = f32[4,128,128]{2,1,0:T(8,128)S(1)} collective-permute-done((f32[4,128,128]{2,1,0:T(8,128)S(1)}, f32[4,128,128]{2,1,0:T(8,128)S(1)}, u32[]{:S(2)}, u32[]{:S(2)}) %collective-permute-start) | collective-permute-done | bytes 262176 | tf_op jit(solution)/shard_map/while/body/eval_jaxpr/ppermute | solution.py:28
  305.8 1.5 collective-permute-start.1
  308.6 1.5 collective-permute-done.1
  310.2 4.0 %collective-permute-done.2 = f32[2,128,128]{2,1,0:T(8,128)S(1)} collective-permute-done((f32[2,128,128]{2,1,0:T(8,128)S(1)}, f32[2,128,128]{2,1,0:T(8,128)S(1)}, u32[]{:S(2)}, u32[]{:S(2)}) %collective-permute-start.2) | collective-permute-done | bytes 131104 | tf_op jit(solution)/shard_map/while/body/eval_jaxpr/ppermute | solution.py:20
  315.8 8.5 %collective-permute-done = f32[4,128,128]{2,1,0:T(8,128)S(1)} collective-permute-done((f32[4,128,128]{2,1,0:T(8,128)S(1)}, f32[4,128,128]{2,1,0:T(8,128)S(1)}, u32[]{:S(2)}, u32[]{:S(2)}) %collective-permute-start) | collective-permute-done | bytes 262176 | tf_op jit(solution)/shard_map/while/body/eval_jaxpr/ppermute | solution.py:28
  327.7 1.5 collective-permute-done.1
  329.3 4.0 %collective-permute-done.2 = f32[2,128,128]{2,1,0:T(8,128)S(1)} collective-permute-done((f32[2,128,128]{2,1,0:T(8,128)S(1)}, f32[2,128,128]{2,1,0:T(8,128)S(1)}, u32[]{:S(2)}, u32[]{:S(2)}) %collective-permute-start.2) | collective-permute-done | bytes 131104 | tf_op jit(solution)/shard_map/while/body/eval_jaxpr/ppermute | solution.py:20
  334.9 8.5 %collective-permute-done = f32[4,128,128]{2,1,0:T(8,128)S(1)} collective-permute-done((f32[4,128,128]{2,1,0:T(8,128)S(1)}, f32[4,128,128]{2,1,0:T(8,128)S(1)}, u32[]{:S(2)}, u32[]{:S(2)}) %collective-permute-start) | collective-permute-done | bytes 262176 | tf_op jit(solution)/shard_map/while/body/eval_jaxpr/ppermute | solution.py:28
  346.8 1.5 collective-permute-done.1
  348.4 4.0 %collective-permute-done.2 = f32[2,128,128]{2,1,0:T(8,128)S(1)} collective-permute-done((f32[2,128,128]{2,1,0:T(8,128)S(1)}, f32[2,128,128]{2,1,0:T(8,128)S(1)}, u32[]{:S(2)}, u32[]{:S(2)}) %collective-permute-start.2) | collective-permute-done | bytes 131104 | tf_op jit(solution)/shard_map/while/body/eval_jaxpr/ppermute | solution.py:20
  354.9 1.5 collective-permute-start.14
  357.7 2.0 collective-permute-done.14
  359.8 4.6 %collective-permute-done.15 = f32[2,128,128]{2,1,0:T(8,128)S(1)} collective-permute-done((f32[2,128,128]{2,1,0:T(8,128)S(1)}, f32[2,128,128]{2,1,0:T(8,128)S(1)}, u32[]{:S(2)}, u32[]{:S(2)}) %collective-permute-start.15) | collective-permute-done | bytes 131104 | tf_op jit(solution)/shard_map/ppermute | solution.py:20
  370.7 4.3 %collective-permute-done.17 = f32[2,128,128]{2,1,0:T(8,128)S(1)} collective-permute-done((f32[2,128,128]{2,1,0:T(8,128)S(1)}, f32[2,128,128]{2,1,0:T(8,128)S(1)}, u32[]{:S(2)}, u32[]{:S(2)}) %collective-permute-start.17) | collective-permute-done | bytes 131104 | tf_op jit(solution)/shard_map/ppermute | solution.py:20
  376.6 1.5 collective-permute-start.18
  380.6 4.4 %collective-permute-done.19 = f32[2,128,128]{2,1,0:T(8,128)S(1)} collective-permute-done((f32[2,128,128]{2,1,0:T(8,128)S(1)}, f32[2,128,128]{2,1,0:T(8,128)S(1)}, u32[]{:S(2)}, u32[]{:S(2)}) %collective-permute-start.19) | collective-permute-done | bytes 131104 | tf_op jit(solution)/shard_map/ppermute | solution.py:20
  (375 shorter events, 108.6 us)
Async XLA Ops:
  1.0 13.2 %collective-permute-start.3 = (f32[2,128,128]{2,1,0:T(8,128)S(1)}, f32[2,128,128]{2,1,0:T(8,128)S(1)}, u32[]{:S(2)}, u32[]{:S(2)}) collective-permute-start(f32[2,128,128]{2,1,0:T(8,128)S(1)} %get-tuple-element.193), channel_id=1, source_target_pairs={{0,1},{2,3},{4,5},{6,7},{8,9},{10,11},{12,13},{14,15},{16,17},{18,... | collective-permute-start | bytes 393224 | tf_op jit(solution)/shard_map/ppermute | solution.py:17
  5.9 8.3 %collective-permute-start.4 = (f32[2,128,128]{2,1,0:T(8,128)S(1)}, f32[2,128,128]{2,1,0:T(8,128)S(1)}, u32[]{:S(2)}, u32[]{:S(2)}) collective-permute-start(f32[2,128,128]{2,1,0:T(8,128)S(1)} %get-tuple-element.194), channel_id=1, source_target_pairs={{1,0},{3,2},{5,4},{7,6},{9,8},{11,10},{13,12},{15,14},{17,16},{19,... | collective-permute-start | bytes 393224 | tf_op jit(solution)/shard_map/ppermute | solution.py:20
  8.3 10.9 %collective-permute-start.5 = (f32[5,1,128,128]{3,2,1,0:T(8,128)S(1)}, f32[5,1,128,128]{3,2,1,0:T(8,128)S(1)}, u32[]{:S(2)}, u32[]{:S(2)}) collective-permute-start(f32[5,1,128,128]{3,2,1,0:T(8,128)S(1)} %get-tuple-element.79), channel_id=1, source_target_pairs={{0,1},{2,3},{4,5},{6,7},{8,9},{10,11},{12,13},{14,15},{16,17},{18,... | collective-permute-start | bytes 983048 | tf_op jit(solution)/shard_map/ppermute | solution.py:17
  12.9 10.5 %collective-permute-start.6 = (f32[5,1,128,128]{3,2,1,0:T(8,128)S(1)}, f32[5,1,128,128]{3,2,1,0:T(8,128)S(1)}, u32[]{:S(2)}, u32[]{:S(2)}) collective-permute-start(f32[5,1,128,128]{3,2,1,0:T(8,128)S(1)} %get-tuple-element.80), channel_id=1, source_target_pairs={{1,0},{3,2},{5,4},{7,6},{9,8},{11,10},{13,12},{15,14},{17,16},{19,... | collective-permute-start | bytes 983048 | tf_op jit(solution)/shard_map/ppermute | solution.py:20
  24.5 19.8 %copy-start = (f32[1,6,128,128]{3,2,1,0:T(8,128)}, f32[1,6,128,128]{3,2,1,0:T(8,128)S(1)}, u32[]{:S(2)}) copy-start(f32[1,6,128,128]{3,2,1,0:T(8,128)S(1)} %get-tuple-element.76) | copy-start | bytes 1179652
  24.5 19.8 %copy-start.3 = (f32[1,6,128,128]{3,2,1,0:T(8,128)}, f32[1,6,128,128]{3,2,1,0:T(8,128)S(1)}, u32[]{:S(2)}) copy-start(f32[1,6,128,128]{3,2,1,0:T(8,128)S(1)} %get-tuple-element.78) | copy-start | bytes 1179652
  24.8 4.0 %collective-permute-start.7 = (f32[2,128,128]{2,1,0:T(8,128)S(1)}, f32[2,128,128]{2,1,0:T(8,128)S(1)}, u32[]{:S(2)}, u32[]{:S(2)}) collective-permute-start(f32[2,128,128]{2,1,0:T(8,128)S(1)} %get-tuple-element.191), channel_id=1, source_target_pairs={{0,1},{2,3},{4,5},{6,7},{8,9},{10,11},{12,13},{14,15},{16,17},{18,... | collective-permute-start | bytes 393224 | tf_op jit(solution)/shard_map/ppermute | solution.py:17
  26.3 6.9 %collective-permute-start.8 = (f32[2,128,128]{2,1,0:T(8,128)S(1)}, f32[2,128,128]{2,1,0:T(8,128)S(1)}, u32[]{:S(2)}, u32[]{:S(2)}) collective-permute-start(f32[2,128,128]{2,1,0:T(8,128)S(1)} %get-tuple-element.192), channel_id=1, source_target_pairs={{1,0},{3,2},{5,4},{7,6},{9,8},{11,10},{13,12},{15,14},{17,16},{19,... | collective-permute-start | bytes 393224 | tf_op jit(solution)/shard_map/ppermute | solution.py:20
  34.7 6.9 %collective-permute-start.10 = (f32[2,128,128]{2,1,0:T(8,128)S(1)}, f32[2,128,128]{2,1,0:T(8,128)S(1)}, u32[]{:S(2)}, u32[]{:S(2)}) collective-permute-start(f32[2,128,128]{2,1,0:T(8,128)S(1)} %get-tuple-element.190), channel_id=1, source_target_pairs={{1,0},{3,2},{5,4},{7,6},{9,8},{11,10},{13,12},{15,14},{17,16},{19,... | collective-permute-start | bytes 393224 | tf_op jit(solution)/shard_map/ppermute | solution.py:20
  36.0 7.1 %collective-permute-start.9 = (f32[2,128,128]{2,1,0:T(8,128)S(1)}, f32[2,128,128]{2,1,0:T(8,128)S(1)}, u32[]{:S(2)}, u32[]{:S(2)}) collective-permute-start(f32[2,128,128]{2,1,0:T(8,128)S(1)} %get-tuple-element.189), channel_id=1, source_target_pairs={{0,1},{2,3},{4,5},{6,7},{8,9},{10,11},{12,13},{14,15},{16,17},{18,... | collective-permute-start | bytes 393224 | tf_op jit(solution)/shard_map/ppermute | solution.py:17
  44.6 8.5 %collective-permute-start.11 = (f32[4,128,128]{2,1,0:T(8,128)S(1)}, f32[4,128,128]{2,1,0:T(8,128)S(1)}, u32[]{:S(2)}, u32[]{:S(2)}) collective-permute-start(f32[4,128,128]{2,1,0:T(8,128)S(1)} %fusion.115), channel_id=1, source_target_pairs={{0,2},{2,4},{4,6},{6,8},{8,10},{10,12},{12,14},{14,16},{16,18},{18... | collective-permute-start | bytes 786440 | tf_op jit(solution)/shard_map/ppermute | solution.py:28
  53.8 7.2 %collective-permute-start.12 = (f32[2,128,128]{2,1,0:T(8,128)}, f32[2,128,128]{2,1,0:T(8,128)S(1)}, u32[]{:S(2)}, u32[]{:S(2)}) collective-permute-start(f32[2,128,128]{2,1,0:T(8,128)} %get-tuple-element.188), channel_id=1, source_target_pairs={{0,1},{2,3},{4,5},{6,7},{8,9},{10,11},{12,13},{14,15},{16,17},{18,... | collective-permute-start | bytes 393224 | tf_op jit(solution)/shard_map/ppermute | solution.py:17
  58.2 6.9 %collective-permute-start.13 = (f32[2,128,128]{2,1,0:T(8,128)S(1)}, f32[2,128,128]{2,1,0:T(8,128)S(1)}, u32[]{:S(2)}, u32[]{:S(2)}) collective-permute-start(f32[2,128,128]{2,1,0:T(8,128)S(1)} %get-tuple-element.187), channel_id=1, source_target_pairs={{1,0},{3,2},{5,4},{7,6},{9,8},{11,10},{13,12},{15,14},{17,16},{19,... | collective-permute-start | bytes 393224 | tf_op jit(solution)/shard_map/ppermute | solution.py:20
  67.4 8.5 %collective-permute-start = (f32[4,128,128]{2,1,0:T(8,128)S(1)}, f32[4,128,128]{2,1,0:T(8,128)S(1)}, u32[]{:S(2)}, u32[]{:S(2)}) collective-permute-start(f32[4,128,128]{2,1,0:T(8,128)S(1)} %get-tuple-element.269), channel_id=1, source_target_pairs={{0,2},{2,4},{4,6},{6,8},{8,10},{10,12},{12,14},{14,16},{16,18},{18... | collective-permute-start | bytes 786440 | tf_op jit(solution)/shard_map/while/body/eval_jaxpr/ppermute | solution.py:28
  76.6 4.3 %collective-permute-start.1 = (f32[2,128,128]{2,1,0:T(8,128)}, f32[2,128,128]{2,1,0:T(8,128)S(1)}, u32[]{:S(2)}, u32[]{:S(2)}) collective-permute-start(f32[2,128,128]{2,1,0:T(8,128)} %get-tuple-element.244), channel_id=1, source_target_pairs={{0,1},{2,3},{4,5},{6,7},{8,9},{10,11},{12,13},{14,15},{16,17},{18,... | collective-permute-start | bytes 393224 | tf_op jit(solution)/shard_map/while/body/eval_jaxpr/ppermute | solution.py:17
  78.1 6.9 %collective-permute-start.2 = (f32[2,128,128]{2,1,0:T(8,128)S(1)}, f32[2,128,128]{2,1,0:T(8,128)S(1)}, u32[]{:S(2)}, u32[]{:S(2)}) collective-permute-start(f32[2,128,128]{2,1,0:T(8,128)S(1)} %get-tuple-element.245), channel_id=1, source_target_pairs={{1,0},{3,2},{5,4},{7,6},{9,8},{11,10},{13,12},{15,14},{17,16},{19,... | collective-permute-start | bytes 393224 | tf_op jit(solution)/shard_map/while/body/eval_jaxpr/ppermute | solution.py:20
  86.5 8.5 %collective-permute-start = (f32[4,128,128]{2,1,0:T(8,128)S(1)}, f32[4,128,128]{2,1,0:T(8,128)S(1)}, u32[]{:S(2)}, u32[]{:S(2)}) collective-permute-start(f32[4,128,128]{2,1,0:T(8,128)S(1)} %get-tuple-element.269), channel_id=1, source_target_pairs={{0,2},{2,4},{4,6},{6,8},{8,10},{10,12},{12,14},{14,16},{16,18},{18... | collective-permute-start | bytes 786440 | tf_op jit(solution)/shard_map/while/body/eval_jaxpr/ppermute | solution.py:28
  95.7 4.3 %collective-permute-start.1 = (f32[2,128,128]{2,1,0:T(8,128)}, f32[2,128,128]{2,1,0:T(8,128)S(1)}, u32[]{:S(2)}, u32[]{:S(2)}) collective-permute-start(f32[2,128,128]{2,1,0:T(8,128)} %get-tuple-element.244), channel_id=1, source_target_pairs={{0,1},{2,3},{4,5},{6,7},{8,9},{10,11},{12,13},{14,15},{16,17},{18,... | collective-permute-start | bytes 393224 | tf_op jit(solution)/shard_map/while/body/eval_jaxpr/ppermute | solution.py:17
  97.2 6.9 %collective-permute-start.2 = (f32[2,128,128]{2,1,0:T(8,128)S(1)}, f32[2,128,128]{2,1,0:T(8,128)S(1)}, u32[]{:S(2)}, u32[]{:S(2)}) collective-permute-start(f32[2,128,128]{2,1,0:T(8,128)S(1)} %get-tuple-element.245), channel_id=1, source_target_pairs={{1,0},{3,2},{5,4},{7,6},{9,8},{11,10},{13,12},{15,14},{17,16},{19,... | collective-permute-start | bytes 393224 | tf_op jit(solution)/shard_map/while/body/eval_jaxpr/ppermute | solution.py:20
  105.6 8.5 %collective-permute-start = (f32[4,128,128]{2,1,0:T(8,128)S(1)}, f32[4,128,128]{2,1,0:T(8,128)S(1)}, u32[]{:S(2)}, u32[]{:S(2)}) collective-permute-start(f32[4,128,128]{2,1,0:T(8,128)S(1)} %get-tuple-element.269), channel_id=1, source_target_pairs={{0,2},{2,4},{4,6},{6,8},{8,10},{10,12},{12,14},{14,16},{16,18},{18... | collective-permute-start | bytes 786440 | tf_op jit(solution)/shard_map/while/body/eval_jaxpr/ppermute | solution.py:28
  114.8 4.3 %collective-permute-start.1 = (f32[2,128,128]{2,1,0:T(8,128)}, f32[2,128,128]{2,1,0:T(8,128)S(1)}, u32[]{:S(2)}, u32[]{:S(2)}) collective-permute-start(f32[2,128,128]{2,1,0:T(8,128)} %get-tuple-element.244), channel_id=1, source_target_pairs={{0,1},{2,3},{4,5},{6,7},{8,9},{10,11},{12,13},{14,15},{16,17},{18,... | collective-permute-start | bytes 393224 | tf_op jit(solution)/shard_map/while/body/eval_jaxpr/ppermute | solution.py:17
  116.3 6.9 %collective-permute-start.2 = (f32[2,128,128]{2,1,0:T(8,128)S(1)}, f32[2,128,128]{2,1,0:T(8,128)S(1)}, u32[]{:S(2)}, u32[]{:S(2)}) collective-permute-start(f32[2,128,128]{2,1,0:T(8,128)S(1)} %get-tuple-element.245), channel_id=1, source_target_pairs={{1,0},{3,2},{5,4},{7,6},{9,8},{11,10},{13,12},{15,14},{17,16},{19,... | collective-permute-start | bytes 393224 | tf_op jit(solution)/shard_map/while/body/eval_jaxpr/ppermute | solution.py:20
  124.7 8.5 %collective-permute-start = (f32[4,128,128]{2,1,0:T(8,128)S(1)}, f32[4,128,128]{2,1,0:T(8,128)S(1)}, u32[]{:S(2)}, u32[]{:S(2)}) collective-permute-start(f32[4,128,128]{2,1,0:T(8,128)S(1)} %get-tuple-element.269), channel_id=1, source_target_pairs={{0,2},{2,4},{4,6},{6,8},{8,10},{10,12},{12,14},{14,16},{16,18},{18... | collective-permute-start | bytes 786440 | tf_op jit(solution)/shard_map/while/body/eval_jaxpr/ppermute | solution.py:28
  133.9 4.3 %collective-permute-start.1 = (f32[2,128,128]{2,1,0:T(8,128)}, f32[2,128,128]{2,1,0:T(8,128)S(1)}, u32[]{:S(2)}, u32[]{:S(2)}) collective-permute-start(f32[2,128,128]{2,1,0:T(8,128)} %get-tuple-element.244), channel_id=1, source_target_pairs={{0,1},{2,3},{4,5},{6,7},{8,9},{10,11},{12,13},{14,15},{16,17},{18,... | collective-permute-start | bytes 393224 | tf_op jit(solution)/shard_map/while/body/eval_jaxpr/ppermute | solution.py:17
  135.4 6.9 %collective-permute-start.2 = (f32[2,128,128]{2,1,0:T(8,128)S(1)}, f32[2,128,128]{2,1,0:T(8,128)S(1)}, u32[]{:S(2)}, u32[]{:S(2)}) collective-permute-start(f32[2,128,128]{2,1,0:T(8,128)S(1)} %get-tuple-element.245), channel_id=1, source_target_pairs={{1,0},{3,2},{5,4},{7,6},{9,8},{11,10},{13,12},{15,14},{17,16},{19,... | collective-permute-start | bytes 393224 | tf_op jit(solution)/shard_map/while/body/eval_jaxpr/ppermute | solution.py:20
  143.8 8.5 %collective-permute-start = (f32[4,128,128]{2,1,0:T(8,128)S(1)}, f32[4,128,128]{2,1,0:T(8,128)S(1)}, u32[]{:S(2)}, u32[]{:S(2)}) collective-permute-start(f32[4,128,128]{2,1,0:T(8,128)S(1)} %get-tuple-element.269), channel_id=1, source_target_pairs={{0,2},{2,4},{4,6},{6,8},{8,10},{10,12},{12,14},{14,16},{16,18},{18... | collective-permute-start | bytes 786440 | tf_op jit(solution)/shard_map/while/body/eval_jaxpr/ppermute | solution.py:28
  153.0 4.3 %collective-permute-start.1 = (f32[2,128,128]{2,1,0:T(8,128)}, f32[2,128,128]{2,1,0:T(8,128)S(1)}, u32[]{:S(2)}, u32[]{:S(2)}) collective-permute-start(f32[2,128,128]{2,1,0:T(8,128)} %get-tuple-element.244), channel_id=1, source_target_pairs={{0,1},{2,3},{4,5},{6,7},{8,9},{10,11},{12,13},{14,15},{16,17},{18,... | collective-permute-start | bytes 393224 | tf_op jit(solution)/shard_map/while/body/eval_jaxpr/ppermute | solution.py:17
  154.5 6.9 %collective-permute-start.2 = (f32[2,128,128]{2,1,0:T(8,128)S(1)}, f32[2,128,128]{2,1,0:T(8,128)S(1)}, u32[]{:S(2)}, u32[]{:S(2)}) collective-permute-start(f32[2,128,128]{2,1,0:T(8,128)S(1)} %get-tuple-element.245), channel_id=1, source_target_pairs={{1,0},{3,2},{5,4},{7,6},{9,8},{11,10},{13,12},{15,14},{17,16},{19,... | collective-permute-start | bytes 393224 | tf_op jit(solution)/shard_map/while/body/eval_jaxpr/ppermute | solution.py:20
  162.9 8.5 %collective-permute-start = (f32[4,128,128]{2,1,0:T(8,128)S(1)}, f32[4,128,128]{2,1,0:T(8,128)S(1)}, u32[]{:S(2)}, u32[]{:S(2)}) collective-permute-start(f32[4,128,128]{2,1,0:T(8,128)S(1)} %get-tuple-element.269), channel_id=1, source_target_pairs={{0,2},{2,4},{4,6},{6,8},{8,10},{10,12},{12,14},{14,16},{16,18},{18... | collective-permute-start | bytes 786440 | tf_op jit(solution)/shard_map/while/body/eval_jaxpr/ppermute | solution.py:28
  172.1 4.3 %collective-permute-start.1 = (f32[2,128,128]{2,1,0:T(8,128)}, f32[2,128,128]{2,1,0:T(8,128)S(1)}, u32[]{:S(2)}, u32[]{:S(2)}) collective-permute-start(f32[2,128,128]{2,1,0:T(8,128)} %get-tuple-element.244), channel_id=1, source_target_pairs={{0,1},{2,3},{4,5},{6,7},{8,9},{10,11},{12,13},{14,15},{16,17},{18,... | collective-permute-start | bytes 393224 | tf_op jit(solution)/shard_map/while/body/eval_jaxpr/ppermute | solution.py:17
  173.6 6.9 %collective-permute-start.2 = (f32[2,128,128]{2,1,0:T(8,128)S(1)}, f32[2,128,128]{2,1,0:T(8,128)S(1)}, u32[]{:S(2)}, u32[]{:S(2)}) collective-permute-start(f32[2,128,128]{2,1,0:T(8,128)S(1)} %get-tuple-element.245), channel_id=1, source_target_pairs={{1,0},{3,2},{5,4},{7,6},{9,8},{11,10},{13,12},{15,14},{17,16},{19,... | collective-permute-start | bytes 393224 | tf_op jit(solution)/shard_map/while/body/eval_jaxpr/ppermute | solution.py:20
  182.0 8.5 %collective-permute-start = (f32[4,128,128]{2,1,0:T(8,128)S(1)}, f32[4,128,128]{2,1,0:T(8,128)S(1)}, u32[]{:S(2)}, u32[]{:S(2)}) collective-permute-start(f32[4,128,128]{2,1,0:T(8,128)S(1)} %get-tuple-element.269), channel_id=1, source_target_pairs={{0,2},{2,4},{4,6},{6,8},{8,10},{10,12},{12,14},{14,16},{16,18},{18... | collective-permute-start | bytes 786440 | tf_op jit(solution)/shard_map/while/body/eval_jaxpr/ppermute | solution.py:28
  191.2 4.3 %collective-permute-start.1 = (f32[2,128,128]{2,1,0:T(8,128)}, f32[2,128,128]{2,1,0:T(8,128)S(1)}, u32[]{:S(2)}, u32[]{:S(2)}) collective-permute-start(f32[2,128,128]{2,1,0:T(8,128)} %get-tuple-element.244), channel_id=1, source_target_pairs={{0,1},{2,3},{4,5},{6,7},{8,9},{10,11},{12,13},{14,15},{16,17},{18,... | collective-permute-start | bytes 393224 | tf_op jit(solution)/shard_map/while/body/eval_jaxpr/ppermute | solution.py:17
  192.7 6.9 %collective-permute-start.2 = (f32[2,128,128]{2,1,0:T(8,128)S(1)}, f32[2,128,128]{2,1,0:T(8,128)S(1)}, u32[]{:S(2)}, u32[]{:S(2)}) collective-permute-start(f32[2,128,128]{2,1,0:T(8,128)S(1)} %get-tuple-element.245), channel_id=1, source_target_pairs={{1,0},{3,2},{5,4},{7,6},{9,8},{11,10},{13,12},{15,14},{17,16},{19,... | collective-permute-start | bytes 393224 | tf_op jit(solution)/shard_map/while/body/eval_jaxpr/ppermute | solution.py:20
  201.1 8.5 %collective-permute-start = (f32[4,128,128]{2,1,0:T(8,128)S(1)}, f32[4,128,128]{2,1,0:T(8,128)S(1)}, u32[]{:S(2)}, u32[]{:S(2)}) collective-permute-start(f32[4,128,128]{2,1,0:T(8,128)S(1)} %get-tuple-element.269), channel_id=1, source_target_pairs={{0,2},{2,4},{4,6},{6,8},{8,10},{10,12},{12,14},{14,16},{16,18},{18... | collective-permute-start | bytes 786440 | tf_op jit(solution)/shard_map/while/body/eval_jaxpr/ppermute | solution.py:28
  210.3 4.3 %collective-permute-start.1 = (f32[2,128,128]{2,1,0:T(8,128)}, f32[2,128,128]{2,1,0:T(8,128)S(1)}, u32[]{:S(2)}, u32[]{:S(2)}) collective-permute-start(f32[2,128,128]{2,1,0:T(8,128)} %get-tuple-element.244), channel_id=1, source_target_pairs={{0,1},{2,3},{4,5},{6,7},{8,9},{10,11},{12,13},{14,15},{16,17},{18,... | collective-permute-start | bytes 393224 | tf_op jit(solution)/shard_map/while/body/eval_jaxpr/ppermute | solution.py:17
  211.8 6.9 %collective-permute-start.2 = (f32[2,128,128]{2,1,0:T(8,128)S(1)}, f32[2,128,128]{2,1,0:T(8,128)S(1)}, u32[]{:S(2)}, u32[]{:S(2)}) collective-permute-start(f32[2,128,128]{2,1,0:T(8,128)S(1)} %get-tuple-element.245), channel_id=1, source_target_pairs={{1,0},{3,2},{5,4},{7,6},{9,8},{11,10},{13,12},{15,14},{17,16},{19,... | collective-permute-start | bytes 393224 | tf_op jit(solution)/shard_map/while/body/eval_jaxpr/ppermute | solution.py:20
  220.2 8.5 %collective-permute-start = (f32[4,128,128]{2,1,0:T(8,128)S(1)}, f32[4,128,128]{2,1,0:T(8,128)S(1)}, u32[]{:S(2)}, u32[]{:S(2)}) collective-permute-start(f32[4,128,128]{2,1,0:T(8,128)S(1)} %get-tuple-element.269), channel_id=1, source_target_pairs={{0,2},{2,4},{4,6},{6,8},{8,10},{10,12},{12,14},{14,16},{16,18},{18... | collective-permute-start | bytes 786440 | tf_op jit(solution)/shard_map/while/body/eval_jaxpr/ppermute | solution.py:28
  229.4 4.3 %collective-permute-start.1 = (f32[2,128,128]{2,1,0:T(8,128)}, f32[2,128,128]{2,1,0:T(8,128)S(1)}, u32[]{:S(2)}, u32[]{:S(2)}) collective-permute-start(f32[2,128,128]{2,1,0:T(8,128)} %get-tuple-element.244), channel_id=1, source_target_pairs={{0,1},{2,3},{4,5},{6,7},{8,9},{10,11},{12,13},{14,15},{16,17},{18,... | collective-permute-start | bytes 393224 | tf_op jit(solution)/shard_map/while/body/eval_jaxpr/ppermute | solution.py:17
  230.9 6.9 %collective-permute-start.2 = (f32[2,128,128]{2,1,0:T(8,128)S(1)}, f32[2,128,128]{2,1,0:T(8,128)S(1)}, u32[]{:S(2)}, u32[]{:S(2)}) collective-permute-start(f32[2,128,128]{2,1,0:T(8,128)S(1)} %get-tuple-element.245), channel_id=1, source_target_pairs={{1,0},{3,2},{5,4},{7,6},{9,8},{11,10},{13,12},{15,14},{17,16},{19,... | collective-permute-start | bytes 393224 | tf_op jit(solution)/shard_map/while/body/eval_jaxpr/ppermute | solution.py:20
  239.3 8.5 %collective-permute-start = (f32[4,128,128]{2,1,0:T(8,128)S(1)}, f32[4,128,128]{2,1,0:T(8,128)S(1)}, u32[]{:S(2)}, u32[]{:S(2)}) collective-permute-start(f32[4,128,128]{2,1,0:T(8,128)S(1)} %get-tuple-element.269), channel_id=1, source_target_pairs={{0,2},{2,4},{4,6},{6,8},{8,10},{10,12},{12,14},{14,16},{16,18},{18... | collective-permute-start | bytes 786440 | tf_op jit(solution)/shard_map/while/body/eval_jaxpr/ppermute | solution.py:28
  248.5 4.3 %collective-permute-start.1 = (f32[2,128,128]{2,1,0:T(8,128)}, f32[2,128,128]{2,1,0:T(8,128)S(1)}, u32[]{:S(2)}, u32[]{:S(2)}) collective-permute-start(f32[2,128,128]{2,1,0:T(8,128)} %get-tuple-element.244), channel_id=1, source_target_pairs={{0,1},{2,3},{4,5},{6,7},{8,9},{10,11},{12,13},{14,15},{16,17},{18,... | collective-permute-start | bytes 393224 | tf_op jit(solution)/shard_map/while/body/eval_jaxpr/ppermute | solution.py:17
  250.0 6.9 %collective-permute-start.2 = (f32[2,128,128]{2,1,0:T(8,128)S(1)}, f32[2,128,128]{2,1,0:T(8,128)S(1)}, u32[]{:S(2)}, u32[]{:S(2)}) collective-permute-start(f32[2,128,128]{2,1,0:T(8,128)S(1)} %get-tuple-element.245), channel_id=1, source_target_pairs={{1,0},{3,2},{5,4},{7,6},{9,8},{11,10},{13,12},{15,14},{17,16},{19,... | collective-permute-start | bytes 393224 | tf_op jit(solution)/shard_map/while/body/eval_jaxpr/ppermute | solution.py:20
  258.4 8.5 %collective-permute-start = (f32[4,128,128]{2,1,0:T(8,128)S(1)}, f32[4,128,128]{2,1,0:T(8,128)S(1)}, u32[]{:S(2)}, u32[]{:S(2)}) collective-permute-start(f32[4,128,128]{2,1,0:T(8,128)S(1)} %get-tuple-element.269), channel_id=1, source_target_pairs={{0,2},{2,4},{4,6},{6,8},{8,10},{10,12},{12,14},{14,16},{16,18},{18... | collective-permute-start | bytes 786440 | tf_op jit(solution)/shard_map/while/body/eval_jaxpr/ppermute | solution.py:28
  267.6 4.3 %collective-permute-start.1 = (f32[2,128,128]{2,1,0:T(8,128)}, f32[2,128,128]{2,1,0:T(8,128)S(1)}, u32[]{:S(2)}, u32[]{:S(2)}) collective-permute-start(f32[2,128,128]{2,1,0:T(8,128)} %get-tuple-element.244), channel_id=1, source_target_pairs={{0,1},{2,3},{4,5},{6,7},{8,9},{10,11},{12,13},{14,15},{16,17},{18,... | collective-permute-start | bytes 393224 | tf_op jit(solution)/shard_map/while/body/eval_jaxpr/ppermute | solution.py:17
  269.1 6.9 %collective-permute-start.2 = (f32[2,128,128]{2,1,0:T(8,128)S(1)}, f32[2,128,128]{2,1,0:T(8,128)S(1)}, u32[]{:S(2)}, u32[]{:S(2)}) collective-permute-start(f32[2,128,128]{2,1,0:T(8,128)S(1)} %get-tuple-element.245), channel_id=1, source_target_pairs={{1,0},{3,2},{5,4},{7,6},{9,8},{11,10},{13,12},{15,14},{17,16},{19,... | collective-permute-start | bytes 393224 | tf_op jit(solution)/shard_map/while/body/eval_jaxpr/ppermute | solution.py:20
  277.5 8.5 %collective-permute-start = (f32[4,128,128]{2,1,0:T(8,128)S(1)}, f32[4,128,128]{2,1,0:T(8,128)S(1)}, u32[]{:S(2)}, u32[]{:S(2)}) collective-permute-start(f32[4,128,128]{2,1,0:T(8,128)S(1)} %get-tuple-element.269), channel_id=1, source_target_pairs={{0,2},{2,4},{4,6},{6,8},{8,10},{10,12},{12,14},{14,16},{16,18},{18... | collective-permute-start | bytes 786440 | tf_op jit(solution)/shard_map/while/body/eval_jaxpr/ppermute | solution.py:28
  286.7 4.3 %collective-permute-start.1 = (f32[2,128,128]{2,1,0:T(8,128)}, f32[2,128,128]{2,1,0:T(8,128)S(1)}, u32[]{:S(2)}, u32[]{:S(2)}) collective-permute-start(f32[2,128,128]{2,1,0:T(8,128)} %get-tuple-element.244), channel_id=1, source_target_pairs={{0,1},{2,3},{4,5},{6,7},{8,9},{10,11},{12,13},{14,15},{16,17},{18,... | collective-permute-start | bytes 393224 | tf_op jit(solution)/shard_map/while/body/eval_jaxpr/ppermute | solution.py:17
  288.2 6.9 %collective-permute-start.2 = (f32[2,128,128]{2,1,0:T(8,128)S(1)}, f32[2,128,128]{2,1,0:T(8,128)S(1)}, u32[]{:S(2)}, u32[]{:S(2)}) collective-permute-start(f32[2,128,128]{2,1,0:T(8,128)S(1)} %get-tuple-element.245), channel_id=1, source_target_pairs={{1,0},{3,2},{5,4},{7,6},{9,8},{11,10},{13,12},{15,14},{17,16},{19,... | collective-permute-start | bytes 393224 | tf_op jit(solution)/shard_map/while/body/eval_jaxpr/ppermute | solution.py:20
  296.6 8.5 %collective-permute-start = (f32[4,128,128]{2,1,0:T(8,128)S(1)}, f32[4,128,128]{2,1,0:T(8,128)S(1)}, u32[]{:S(2)}, u32[]{:S(2)}) collective-permute-start(f32[4,128,128]{2,1,0:T(8,128)S(1)} %get-tuple-element.269), channel_id=1, source_target_pairs={{0,2},{2,4},{4,6},{6,8},{8,10},{10,12},{12,14},{14,16},{16,18},{18... | collective-permute-start | bytes 786440 | tf_op jit(solution)/shard_map/while/body/eval_jaxpr/ppermute | solution.py:28
  305.8 4.3 %collective-permute-start.1 = (f32[2,128,128]{2,1,0:T(8,128)}, f32[2,128,128]{2,1,0:T(8,128)S(1)}, u32[]{:S(2)}, u32[]{:S(2)}) collective-permute-start(f32[2,128,128]{2,1,0:T(8,128)} %get-tuple-element.244), channel_id=1, source_target_pairs={{0,1},{2,3},{4,5},{6,7},{8,9},{10,11},{12,13},{14,15},{16,17},{18,... | collective-permute-start | bytes 393224 | tf_op jit(solution)/shard_map/while/body/eval_jaxpr/ppermute | solution.py:17
  307.3 6.9 %collective-permute-start.2 = (f32[2,128,128]{2,1,0:T(8,128)S(1)}, f32[2,128,128]{2,1,0:T(8,128)S(1)}, u32[]{:S(2)}, u32[]{:S(2)}) collective-permute-start(f32[2,128,128]{2,1,0:T(8,128)S(1)} %get-tuple-element.245), channel_id=1, source_target_pairs={{1,0},{3,2},{5,4},{7,6},{9,8},{11,10},{13,12},{15,14},{17,16},{19,... | collective-permute-start | bytes 393224 | tf_op jit(solution)/shard_map/while/body/eval_jaxpr/ppermute | solution.py:20
  315.7 8.5 %collective-permute-start = (f32[4,128,128]{2,1,0:T(8,128)S(1)}, f32[4,128,128]{2,1,0:T(8,128)S(1)}, u32[]{:S(2)}, u32[]{:S(2)}) collective-permute-start(f32[4,128,128]{2,1,0:T(8,128)S(1)} %get-tuple-element.269), channel_id=1, source_target_pairs={{0,2},{2,4},{4,6},{6,8},{8,10},{10,12},{12,14},{14,16},{16,18},{18... | collective-permute-start | bytes 786440 | tf_op jit(solution)/shard_map/while/body/eval_jaxpr/ppermute | solution.py:28
  324.9 4.3 %collective-permute-start.1 = (f32[2,128,128]{2,1,0:T(8,128)}, f32[2,128,128]{2,1,0:T(8,128)S(1)}, u32[]{:S(2)}, u32[]{:S(2)}) collective-permute-start(f32[2,128,128]{2,1,0:T(8,128)} %get-tuple-element.244), channel_id=1, source_target_pairs={{0,1},{2,3},{4,5},{6,7},{8,9},{10,11},{12,13},{14,15},{16,17},{18,... | collective-permute-start | bytes 393224 | tf_op jit(solution)/shard_map/while/body/eval_jaxpr/ppermute | solution.py:17
  326.4 6.9 %collective-permute-start.2 = (f32[2,128,128]{2,1,0:T(8,128)S(1)}, f32[2,128,128]{2,1,0:T(8,128)S(1)}, u32[]{:S(2)}, u32[]{:S(2)}) collective-permute-start(f32[2,128,128]{2,1,0:T(8,128)S(1)} %get-tuple-element.245), channel_id=1, source_target_pairs={{1,0},{3,2},{5,4},{7,6},{9,8},{11,10},{13,12},{15,14},{17,16},{19,... | collective-permute-start | bytes 393224 | tf_op jit(solution)/shard_map/while/body/eval_jaxpr/ppermute | solution.py:20
  334.8 8.5 %collective-permute-start = (f32[4,128,128]{2,1,0:T(8,128)S(1)}, f32[4,128,128]{2,1,0:T(8,128)S(1)}, u32[]{:S(2)}, u32[]{:S(2)}) collective-permute-start(f32[4,128,128]{2,1,0:T(8,128)S(1)} %get-tuple-element.269), channel_id=1, source_target_pairs={{0,2},{2,4},{4,6},{6,8},{8,10},{10,12},{12,14},{14,16},{16,18},{18... | collective-permute-start | bytes 786440 | tf_op jit(solution)/shard_map/while/body/eval_jaxpr/ppermute | solution.py:28
  344.0 4.3 %collective-permute-start.1 = (f32[2,128,128]{2,1,0:T(8,128)}, f32[2,128,128]{2,1,0:T(8,128)S(1)}, u32[]{:S(2)}, u32[]{:S(2)}) collective-permute-start(f32[2,128,128]{2,1,0:T(8,128)} %get-tuple-element.244), channel_id=1, source_target_pairs={{0,1},{2,3},{4,5},{6,7},{8,9},{10,11},{12,13},{14,15},{16,17},{18,... | collective-permute-start | bytes 393224 | tf_op jit(solution)/shard_map/while/body/eval_jaxpr/ppermute | solution.py:17
  345.5 6.9 %collective-permute-start.2 = (f32[2,128,128]{2,1,0:T(8,128)S(1)}, f32[2,128,128]{2,1,0:T(8,128)S(1)}, u32[]{:S(2)}, u32[]{:S(2)}) collective-permute-start(f32[2,128,128]{2,1,0:T(8,128)S(1)} %get-tuple-element.245), channel_id=1, source_target_pairs={{1,0},{3,2},{5,4},{7,6},{9,8},{11,10},{13,12},{15,14},{17,16},{19,... | collective-permute-start | bytes 393224 | tf_op jit(solution)/shard_map/while/body/eval_jaxpr/ppermute | solution.py:20
  354.9 4.8 %collective-permute-start.14 = (f32[2,128,128]{2,1,0:T(8,128)S(1)}, f32[2,128,128]{2,1,0:T(8,128)S(1)}, u32[]{:S(2)}, u32[]{:S(2)}) collective-permute-start(f32[2,128,128]{2,1,0:T(8,128)S(1)} %get-tuple-element.185), channel_id=1, source_target_pairs={{0,1},{2,3},{4,5},{6,7},{8,9},{10,11},{12,13},{14,15},{16,17},{18,... | collective-permute-start | bytes 393224 | tf_op jit(solution)/shard_map/ppermute | solution.py:17
  356.4 7.9 %collective-permute-start.15 = (f32[2,128,128]{2,1,0:T(8,128)S(1)}, f32[2,128,128]{2,1,0:T(8,128)S(1)}, u32[]{:S(2)}, u32[]{:S(2)}) collective-permute-start(f32[2,128,128]{2,1,0:T(8,128)S(1)} %get-tuple-element.186), channel_id=1, source_target_pairs={{1,0},{3,2},{5,4},{7,6},{9,8},{11,10},{13,12},{15,14},{17,16},{19,... | collective-permute-start | bytes 393224 | tf_op jit(solution)/shard_map/ppermute | solution.py:20
  366.7 4.0 %collective-permute-start.16 = (f32[2,128,128]{2,1,0:T(8,128)S(1)}, f32[2,128,128]{2,1,0:T(8,128)S(1)}, u32[]{:S(2)}, u32[]{:S(2)}) collective-permute-start(f32[2,128,128]{2,1,0:T(8,128)S(1)} %get-tuple-element.183), channel_id=1, source_target_pairs={{0,1},{2,3},{4,5},{6,7},{8,9},{10,11},{12,13},{14,15},{16,17},{18,... | collective-permute-start | bytes 393224 | tf_op jit(solution)/shard_map/ppermute | solution.py:17
  368.2 6.9 %collective-permute-start.17 = (f32[2,128,128]{2,1,0:T(8,128)S(1)}, f32[2,128,128]{2,1,0:T(8,128)S(1)}, u32[]{:S(2)}, u32[]{:S(2)}) collective-permute-start(f32[2,128,128]{2,1,0:T(8,128)S(1)} %get-tuple-element.184), channel_id=1, source_target_pairs={{1,0},{3,2},{5,4},{7,6},{9,8},{11,10},{13,12},{15,14},{17,16},{19,... | collective-permute-start | bytes 393224 | tf_op jit(solution)/shard_map/ppermute | solution.py:20
  376.6 4.0 %collective-permute-start.18 = (f32[2,128,128]{2,1,0:T(8,128)S(1)}, f32[2,128,128]{2,1,0:T(8,128)S(1)}, u32[]{:S(2)}, u32[]{:S(2)}) collective-permute-start(f32[2,128,128]{2,1,0:T(8,128)S(1)} %get-tuple-element.181), channel_id=1, source_target_pairs={{0,1},{2,3},{4,5},{6,7},{8,9},{10,11},{12,13},{14,15},{16,17},{18,... | collective-permute-start | bytes 393224 | tf_op jit(solution)/shard_map/ppermute | solution.py:17
  378.1 6.9 %collective-permute-start.19 = (f32[2,128,128]{2,1,0:T(8,128)S(1)}, f32[2,128,128]{2,1,0:T(8,128)S(1)}, u32[]{:S(2)}, u32[]{:S(2)}) collective-permute-start(f32[2,128,128]{2,1,0:T(8,128)S(1)} %get-tuple-element.182), channel_id=1, source_target_pairs={{1,0},{3,2},{5,4},{7,6},{9,8},{11,10},{13,12},{15,14},{17,16},{19,... | collective-permute-start | bytes 393224 | tf_op jit(solution)/shard_map/ppermute | solution.py:20
  (7 other events, 36.3 us)
where the time goes:
time: 389 us; the launch traced here: 388 us
  waiting for transfers between devices  259 us (67%)
  starting transfers between devices  77.1 us (20%)
  local copies, waits for them, and re-layouts  30.3 us (8%)
  other arithmetic  19.3 us (5%)
    ppermute x16, waiting for transfers between devices, shifted(): return lax.ppermute(value, axis, pairs)  136 us
    ppermute x23, waiting for transfers between devices, extended(): lax.ppermute(lax.slice_in_dim(block, 0, width, axis=dim), axis, backward)  86.9 us
    ppermute x23, starting transfers between devices, extended(): lax.ppermute(lax.slice_in_dim(block, block.shape[dim] - width, None, axis...  46.4 us
    ppermute x23, waiting for transfers between devices, extended(): lax.ppermute(lax.slice_in_dim(block, block.shape[dim] - width, None, axis...  35.9 us
    ppermute x23, starting transfers between devices, extended(): lax.ppermute(lax.slice_in_dim(block, 0, width, axis=dim), axis, backward)  29.7 us
    slice x88, local copies, waits for them, and re-layouts, neighbours(): return total + jnp.roll(middle, 1, axis=2) + jnp.roll(middle, -1, axis=2)  13.8 us
    slice x16, local copies, waits for them, and re-layouts, extended(): lax.slice_in_dim(block, 0, width, axis=dim)  11 us
    div x27, other arithmetic, sweep_once(): return (target + weight * neighbours(field)) / scaled  10.5 us
  transfers between devices with their start and end apart: 62, of which 60 were waited for; matrix products, arithmetic and copies ran while one was open for 1% of the time, Pallas kernels for 0%

commit v1 on v0

v1 whole, which is shorter than its diff:
```python
import functools

import jax
import jax.numpy as jnp
from jax import lax
from jax.experimental import pallas as pl
from jax.experimental.pallas import tpu as pltpu
from jax.sharding import PartitionSpec as P

step_length = 0.1
MESH = pl.DeviceIdType.MESH
SUB = 8


def kernel(nt, ns, cf, zl, sx, forcing, kappa_in, guess_in, out,
           kap, gue, src, cur, mid, tot, bef, anc, slots, tgt, wf, wc, stage,
           loc_sem, send_sem, recv_sem, tm_send, tm_recv, an_send, an_recv, out_sem):
    rows = sx // SUB
    nz = ns * zl
    k = lax.axis_index("tm")
    h = lax.axis_index("space")
    owner = lax.rem(k, ns)
    active = h == owner
    shifts = []
    step = 1
    while step < nt:
        shifts.append(step)
        step *= 2
    offsets = sorted({o % nt for s in shifts for o in (s, -s)} - {0})

    barrier = pltpu.get_barrier_semaphore()
    for d in range(1, ns):
        pl.semaphore_signal(barrier, inc=1, device_id=(k, lax.rem(h + d, ns)), device_id_type=MESH)

    @pl.when(active)
    def _():
        for o in offsets:
            kk = lax.rem(k + o, nt)
            pl.semaphore_signal(barrier, inc=1, device_id=(kk, lax.rem(kk, ns)), device_id_type=MESH)

    own = pl.ds(h * zl, zl)
    local = [pltpu.make_async_copy(kappa_in, kap.at[own], loc_sem.at[0]),
             pltpu.make_async_copy(guess_in.at[0], gue.at[own], loc_sem.at[1])]
    for j in range(cf):
        local.append(pltpu.make_async_copy(forcing.at[j], src.at[j, own], loc_sem.at[2 + j]))
    for copy in local:
        copy.start()

    @pl.when(active)
    def _():
        pl.semaphore_wait(barrier, ns - 1 + len(offsets))

    @pl.when(jnp.logical_not(active))
    def _():
        pl.semaphore_wait(barrier, ns - 1)

    def piece(a, d, sender, target):
        planes = pl.ds(sender * zl, zl)
        if a == 0:
            s, t = kappa_in, kap.at[planes]
        elif a == 1:
            s, t = guess_in.at[0], gue.at[planes]
        else:
            s, t = forcing.at[a - 2], src.at[a - 2, planes]
        return pltpu.make_async_remote_copy(
            src_ref=s, dst_ref=t, send_sem=send_sem.at[a, d], recv_sem=recv_sem.at[a, d],
            device_id=(k, target), device_id_type=MESH)

    first = [0, 1] + [2 + j for j in range(1, cf)] + [2]
    second = [0] + [2 + j for j in range(1, cf)]

    def send_first():
        for d in range(1, ns):
            target = lax.rem(h + d, ns)

            @pl.when(target == owner)
            def _():
                for a in first:
                    piece(a, d, h, target).start()

    def send_second():
        for d in range(1, ns):
            target = lax.rem(h + d, ns)

            @pl.when(target != owner)
            def _():
                for a in second:
                    piece(a, d, h, target).start()

    def arrive(a):
        for d in range(1, ns):
            piece(a, d, lax.rem(h + ns - d, ns), h).wait_recv()

    def planes_loop(body):
        lax.fori_loop(0, nz, lambda z, c: (body(z), c)[1], 0)

    def natural(ref, z, r):
        return ref[z, pl.ds(r, SUB, stride=rows), :]

    def sums(f, z):
        c = [f[z + 1, r] for r in range(rows)]
        res = []
        for r in range(rows):
            lo = c[r - 1] if r > 0 else pltpu.roll(c[rows - 1], 1, 0)
            hi = c[r + 1] if r < rows - 1 else pltpu.roll(c[0], SUB - 1, 0)
            n = (f[z, r] + f[z + 2, r]) + (lo + hi)
            width = c[r].shape[1]
            res.append(n + (pltpu.roll(c[r], 1, 1) + pltpu.roll(c[r], width - 1, 1)))
        return c, res

    def step_of(f, w, source):
        def one(z):
            c, n = sums(f, z)
            for r in range(rows):
                wr = w[z, r]
                b = c[r]
                if source is not None:
                    b = b + step_length * natural(source, z, r)
                t = b - (6.0 * wr) * b
                tgt[z, r] = t
                mid[z + 1, r] = t + wr * n[r]

        def two(z):
            _, n = sums(mid, z)
            for r in range(rows):
                f[z + 1, r] = tgt[z, r] + w[z, r] * n[r]

        planes_loop(one)
        planes_loop(two)

    def zero_ends(ref):
        zero = jnp.zeros(ref.shape[1:], jnp.float32)
        ref[0] = zero
        ref[nz + 1] = zero

    def weights():
        def body(z):
            for r in range(rows):
                kp = natural(kap, z, r)
                a = step_length * kp
                wf[z, r] = a / (1.0 + 6.0 * a)
                b = (cf * step_length) * kp
                wc[z, r] = b / (1.0 + 6.0 * b)
        planes_loop(body)

    def shift(i, s, source, target):
        kk = lax.rem(k + s, nt)
        return pltpu.make_async_remote_copy(
            src_ref=source.at[pl.ds(1, nz)], dst_ref=target.at[pl.ds(1, nz)],
            send_sem=tm_send.at[i], recv_sem=tm_recv.at[i],
            device_id=(kk, lax.rem(kk, ns)), device_id_type=MESH)

    def anchor_copy(d, target):
        return pltpu.make_async_remote_copy(
            src_ref=anc.at[pl.ds(1, nz)], dst_ref=anc.at[pl.ds(1, nz)],
            send_sem=an_send.at[d], recv_sem=an_recv.at[d],
            device_id=(k, target), device_id_type=MESH)

    send_first()

    @pl.when(jnp.logical_not(active))
    def _():
        send_second()

    zero_ends(mid)
    zero_ends(anc)
    for copy in local:
        copy.wait()

    @pl.when(active)
    def _():
        zero_ends(cur)
        zero_ends(bef)
        for i in range(len(shifts)):
            zero_ends(slots.at[i])
        arrive(0)
        weights()
        arrive(1)

        def load(z):
            for r in range(rows):
                cur[z + 1, r] = natural(gue, z, r)

        planes_loop(load)
        for j in range(1, cf):
            arrive(2 + j)
            step_of(cur, wf, src.at[j])
        move = shift(0, 1, cur, bef)
        move.start()
        arrive(2)
        move.wait()
        step_of(bef, wf, src.at[0])

        def defect(z):
            for r in range(rows):
                tot[z + 1, r] = bef[z + 1, r] - natural(gue, z, r)

        planes_loop(defect)
        for i, s in enumerate(shifts):
            slot = slots.at[i]
            move = shift(1 + i, s, tot, slot)
            move.start()
            move.wait_recv()
            if i == 0:
                send_second()

            def again(n, c):
                step_of(slot, wc, None)
                return c

            lax.fori_loop(0, s, again, 0)
            move.wait_send()
            last = i == len(shifts) - 1

            def add(z):
                for r in range(rows):
                    v = tot[z + 1, r] + slot[z + 1, r]
                    if last:
                        anc[z + 1, r] = v + natural(gue, z, r)
                    else:
                        tot[z + 1, r] = v

            planes_loop(add)
        for d in range(1, ns):
            anchor_copy(d, lax.rem(h + d, ns)).start()

    @pl.when(jnp.logical_not(active))
    def _():
        for a in second:
            arrive(a)
        weights()
        for d in range(1, ns):
            @pl.when(lax.rem(h + ns - d, ns) == owner)
            def _():
                anchor_copy(d, h).wait_recv()

    @pl.when(active)
    def _():
        for d in range(1, ns):
            anchor_copy(d, lax.rem(h + d, ns)).wait_send()

    results = []
    for j in range(cf):
        if j > 0:
            step_of(anc, wf, src.at[j])

        def put(z, c):
            for r in range(rows):
                stage[j, z, pl.ds(r, SUB, stride=rows), :] = anc[h * zl + z + 1, r]
            return c

        lax.fori_loop(0, zl, put, 0)
        copy = pltpu.make_async_copy(stage.at[j], out.at[j], out_sem.at[j])
        copy.start()
        results.append(copy)
    for d in range(1, ns):
        target = lax.rem(h + d, ns)

        @pl.when(target == owner)
        def _():
            for a in first:
                piece(a, d, h, target).wait_send()

        @pl.when(target != owner)
        def _():
            for a in second:
                piece(a, d, h, target).wait_send()
    for copy in results:
        copy.wait()


def per_device(nt, ns, forcing, conductivity, guess):
    cf, zl, sx, sy = forcing.shape
    nz = zl * ns
    rows = sx // SUB
    hops = max(1, (nt - 1).bit_length())
    f32 = jnp.float32
    field = pltpu.VMEM((nz + 2, rows, SUB, sy), f32)
    inner = pltpu.VMEM((nz, rows, SUB, sy), f32)
    plain = pltpu.VMEM((nz, sx, sy), f32)
    dma = pltpu.SemaphoreType.DMA
    return pl.pallas_call(
        functools.partial(kernel, nt, ns, cf, zl, sx),
        out_shape=jax.ShapeDtypeStruct(forcing.shape, f32),
        in_specs=[pl.BlockSpec(memory_space=pl.ANY)] * 3,
        out_specs=pl.BlockSpec(memory_space=pl.ANY),
        scratch_shapes=[
            plain, plain, pltpu.VMEM((cf, nz, sx, sy), f32),
            field, field, field, field, field,
            pltpu.VMEM((hops, nz + 2, rows, SUB, sy), f32),
            inner, inner, inner,
            pltpu.VMEM((cf, zl, sx, sy), f32),
            dma((cf + 2,)), dma((cf + 2, ns)), dma((cf + 2, ns)),
            dma((hops + 1,)), dma((hops + 1,)), dma((ns,)), dma((ns,)), dma((cf,)),
        ],
        compiler_params=pltpu.CompilerParams(
            collective_id=0, has_side_effects=True, vmem_limit_bytes=56 * 1024 * 1024),
    )(forcing, conductivity, guess)


def solution(mesh):
    in_specs = (P("tm", "space", None, None), P("space", None, None), P("tm", "space", None, None))
    return jax.shard_map(
        functools.partial(per_device, mesh.shape["tm"], mesh.shape["space"]),
        mesh=mesh, in_specs=in_specs, out_specs=P("tm", "space", None, None), check_vma=False)
```

time: 389 us -> 111 us (0.29)
  waiting for transfers between devices: 259 us -> 0 us
  Pallas kernels: 0 us -> 108 us
  starting transfers between devices: 77.1 us -> 0 us
  local copies, waits for them, and re-layouts: 30.3 us -> 2.3 us
  other arithmetic: 19.3 us -> 0 us
    ppermute x62 -> x0, waiting for transfers between devices: 259 us -> none  [the longest x16 136 us: shifted(): return lax.ppermute(value, axis, pairs)]
    pallas_call x0 -> x1, Pallas kernels: none -> 108 us  [per_device(): pl.pallas_call(functools.partial(kernel, nt, ns, cf, zl, sx), out_shape=j...]
    ppermute x62 -> x0, starting transfers between devices: 77.1 us -> none  [the longest x23 46.4 us: extended(): lax.ppermute(lax.slice_in_dim(block, block.shape[dim] - width, None, axis...]
    slice x192 -> x0, local copies, waits for them, and re-layouts: 28.1 us -> none  [the longest x88 13.8 us: neighbours(): return total + jnp.roll(middle, 1, axis=2) + jnp.roll(middle, -1, axis=2)]
    div x27 -> x0, other arithmetic: 10.5 us -> none  [sweep_once(): return (target + weight * neighbours(field)) / scaled]
    add x17 -> x0, other arithmetic: 5.76 us -> none  [the longest x15 4.65 us: relay(): return defect + coarse_step(moved)]
  transfers between devices with their start and end apart: 62 -> 0, of which waited for: 60 -> 0; matrix products, arithmetic and copies ran while one was open for 1% -> 0% of each run, Pallas kernels for 0% -> 0%
where the time goes in v1:
time: 111 us; the launch traced here: 110 us
  Pallas kernels  108 us (97%)
  local copies, waits for them, and re-layouts  2.3 us (2%)
    pallas_call x1, Pallas kernels, per_device(): pl.pallas_call(functools.partial(kernel, nt, ns, cf, zl, sx), out_shape=j...  108 us
    unnamed x1, local copies, waits for them, and re-layouts  2.3 us

profile of v1, /device:TPU:0, one launch (start us, length us, event | category | flops | bytes accessed | tf_op | source)
XLA Modules:
  0.0 110.3 jit_solution(16087579422007602980)
XLA Ops:
  0.0 108.0 %shard_map.37 = f32[4,4,128,128]{3,2,1,0:T(8,128)} custom-call(f32[4,4,128,128]{3,2,1,0:T(8,128)} %forcing.1, f32[4,128,128]{2,1,0:T(8,128)} %kappa_in.1, f32[1,4,128,128]{3,2,1,0:T(8,128)} %guess_in.1), custom_call_target="tpu_custom_call" | custom-call | tf_op jit(solution)/shard_map/pallas_call | solution.py:282
  108.0 2.3 %copy.5 = f32[4,4,128,128]{3,2,1,0:T(8,128)} copy(f32[4,4,128,128]{3,2,1,0:T(8,128)} %shard_map.37) | data formatting | bytes 2097152

commit v2 on v1

--- a/solution.py
+++ b/solution.py
@@ -10,6 +10,8 @@
 step_length = 0.1
 MESH = pl.DeviceIdType.MESH
 SUB = 8
+UNROLL = 8
+PARTS = 1
 
 
 def kernel(nt, ns, cf, zl, sx, forcing, kappa_in, guess_in, out,
@@ -75,7 +77,9 @@
 
             @pl.when(target == owner)
             def _():
-                for a in first:
+                for n, a in enumerate(first):
+                    if n > 1:
+                        piece(first[n - 2], d, h, target).wait_send()
                     piece(a, d, h, target).start()
 
     def send_second():
@@ -92,38 +96,44 @@
             piece(a, d, lax.rem(h + ns - d, ns), h).wait_recv()
 
     def planes_loop(body):
-        lax.fori_loop(0, nz, lambda z, c: (body(z), c)[1], 0)
+        def group(g, c):
+            for u in range(UNROLL):
+                body(g * UNROLL + u)
+            return c
+
+        if nz == UNROLL:
+            group(0, 0)
+        else:
+            whole = nz // UNROLL
+            lax.fori_loop(0, whole, group, 0)
+            for z in range(whole * UNROLL, nz):
+                body(z)
 
     def natural(ref, z, r):
         return ref[z, pl.ds(r, SUB, stride=rows), :]
 
-    def sums(f, z):
-        c = [f[z + 1, r] for r in range(rows)]
-        res = []
-        for r in range(rows):
-            lo = c[r - 1] if r > 0 else pltpu.roll(c[rows - 1], 1, 0)
-            hi = c[r + 1] if r < rows - 1 else pltpu.roll(c[0], SUB - 1, 0)
-            n = (f[z, r] + f[z + 2, r]) + (lo + hi)
-            width = c[r].shape[1]
-            res.append(n + (pltpu.roll(c[r], 1, 1) + pltpu.roll(c[r], width - 1, 1)))
-        return c, res
+    def total(f, z, r):
+        c = f[z + 1, r]
+        lo = f[z + 1, r - 1] if r > 0 else pltpu.roll(f[z + 1, rows - 1], 1, 0)
+        hi = f[z + 1, r + 1] if r < rows - 1 else pltpu.roll(f[z + 1, 0], SUB - 1, 0)
+        side = pltpu.roll(c, 1, 1) + pltpu.roll(c, c.shape[1] - 1, 1)
+        return c, ((f[z, r] + f[z + 2, r]) + (lo + hi)) + side
 
     def step_of(f, w, source):
         def one(z):
-            c, n = sums(f, z)
-            for r in range(rows):
+            for r in range(rows):
+                b, n = total(f, z, r)
                 wr = w[z, r]
-                b = c[r]
                 if source is not None:
                     b = b + step_length * natural(source, z, r)
                 t = b - (6.0 * wr) * b
                 tgt[z, r] = t
-                mid[z + 1, r] = t + wr * n[r]
+                mid[z + 1, r] = t + wr * n
 
         def two(z):
-            _, n = sums(mid, z)
-            for r in range(rows):
-                f[z + 1, r] = tgt[z, r] + w[z, r] * n[r]
+            for r in range(rows):
+                _, n = total(mid, z, r)
+                f[z + 1, r] = tgt[z, r] + w[z, r] * n
 
         planes_loop(one)
         planes_loop(two)
@@ -143,18 +153,34 @@
                 wc[z, r] = b / (1.0 + 6.0 * b)
         planes_loop(body)
 
+    part = nz // PARTS
+
     def shift(i, s, source, target):
         kk = lax.rem(k + s, nt)
-        return pltpu.make_async_remote_copy(
-            src_ref=source.at[pl.ds(1, nz)], dst_ref=target.at[pl.ds(1, nz)],
-            send_sem=tm_send.at[i], recv_sem=tm_recv.at[i],
-            device_id=(kk, lax.rem(kk, ns)), device_id_type=MESH)
+        return [pltpu.make_async_remote_copy(
+            src_ref=source.at[pl.ds(1 + q * part, part)],
+            dst_ref=target.at[pl.ds(1 + q * part, part)],
+            send_sem=tm_send.at[i, q], recv_sem=tm_recv.at[i, q],
+            device_id=(kk, lax.rem(kk, ns)), device_id_type=MESH) for q in range(PARTS)]
 
     def anchor_copy(d, target):
-        return pltpu.make_async_remote_copy(
-            src_ref=anc.at[pl.ds(1, nz)], dst_ref=anc.at[pl.ds(1, nz)],
-            send_sem=an_send.at[d], recv_sem=an_recv.at[d],
-            device_id=(k, target), device_id_type=MESH)
+        return [pltpu.make_async_remote_copy(
+            src_ref=anc.at[pl.ds(1 + q * part, part)],
+            dst_ref=anc.at[pl.ds(1 + q * part, part)],
+            send_sem=an_send.at[d, q], recv_sem=an_recv.at[d, q],
+            device_id=(k, target), device_id_type=MESH) for q in range(PARTS)]
+
+    def start(copies):
+        for one in copies:
+            one.start()
+
+    def wait_recv(copies):
+        for one in copies:
+            one.wait_recv()
+
+    def wait_send(copies):
+        for one in copies:
+            one.wait_send()
 
     send_first()
 
@@ -186,9 +212,10 @@
             arrive(2 + j)
             step_of(cur, wf, src.at[j])
         move = shift(0, 1, cur, bef)
-        move.start()
+        start(move)
         arrive(2)
-        move.wait()
+        wait_recv(move)
+        wait_send(move)
         step_of(bef, wf, src.at[0])
 
         def defect(z):
@@ -199,8 +226,8 @@
         for i, s in enumerate(shifts):
             slot = slots.at[i]
             move = shift(1 + i, s, tot, slot)
-            move.start()
-            move.wait_recv()
+            start(move)
+            wait_recv(move)
             if i == 0:
                 send_second()
 
@@ -209,7 +236,7 @@
                 return c
 
             lax.fori_loop(0, s, again, 0)
-            move.wait_send()
+            wait_send(move)
             last = i == len(shifts) - 1
 
             def add(z):
@@ -222,7 +249,7 @@
 
             planes_loop(add)
         for d in range(1, ns):
-            anchor_copy(d, lax.rem(h + d, ns)).start()
+            start(anchor_copy(d, lax.rem(h + d, ns)))
 
     @pl.when(jnp.logical_not(active))
     def _():
@@ -232,12 +259,12 @@
         for d in range(1, ns):
             @pl.when(lax.rem(h + ns - d, ns) == owner)
             def _():
-                anchor_copy(d, h).wait_recv()
+                wait_recv(anchor_copy(d, h))
 
     @pl.when(active)
     def _():
         for d in range(1, ns):
-            anchor_copy(d, lax.rem(h + d, ns)).wait_send()
+            wait_send(anchor_copy(d, lax.rem(h + d, ns)))
 
     results = []
     for j in range(cf):
@@ -258,7 +285,7 @@
 
         @pl.when(target == owner)
         def _():
-            for a in first:
+            for a in first[-2:]:
                 piece(a, d, h, target).wait_send()
 
         @pl.when(target != owner)
@@ -291,7 +318,8 @@
             inner, inner, inner,
             pltpu.VMEM((cf, zl, sx, sy), f32),
             dma((cf + 2,)), dma((cf + 2, ns)), dma((cf + 2, ns)),
-            dma((hops + 1,)), dma((hops + 1,)), dma((ns,)), dma((ns,)), dma((cf,)),
+            dma((hops + 1, PARTS)), dma((hops + 1, PARTS)),
+            dma((ns, PARTS)), dma((ns, PARTS)), dma((cf,)),
         ],
         compiler_params=pltpu.CompilerParams(
             collective_id=0, has_side_effects=True, vmem_limit_bytes=56 * 1024 * 1024),

time: 111 us -> 89.8 us (0.81)
  Pallas kernels: 108 us -> 86.6 us
    pallas_call x1, Pallas kernels: 108 us -> 86.6 us  [per_device(): pl.pallas_call(functools.partial(kernel, nt, ns, cf, zl, sx), out_shape=j...]
where the time goes in v2:
time: 89.8 us; the launch traced here: 88.9 us
  Pallas kernels  86.6 us (96%)
  local copies, waits for them, and re-layouts  2.3 us (3%)
    pallas_call x1, Pallas kernels, per_device(): pl.pallas_call(functools.partial(kernel, nt, ns, cf, zl, sx), out_shape=j...  86.6 us
    unnamed x1, local copies, waits for them, and re-layouts  2.3 us

profile of v2, /device:TPU:0, one launch (start us, length us, event | category | flops | bytes accessed | tf_op | source)
XLA Modules:
  0.0 88.9 jit_solution(6739485992989481899)
XLA Ops:
  0.0 86.6 %shard_map.37 = f32[4,4,128,128]{3,2,1,0:T(8,128)} custom-call(f32[4,4,128,128]{3,2,1,0:T(8,128)} %forcing.1, f32[4,128,128]{2,1,0:T(8,128)} %kappa_in.1, f32[1,4,128,128]{3,2,1,0:T(8,128)} %guess_in.1), custom_call_target="tpu_custom_call" | custom-call | tf_op jit(solution)/shard_map/pallas_call | solution.py:309
  86.6 2.3 %copy.5 = f32[4,4,128,128]{3,2,1,0:T(8,128)} copy(f32[4,4,128,128]{3,2,1,0:T(8,128)} %shard_map.37) | data formatting | bytes 2097152
